TPU v7x, 32 devices: a whole 2x2x4 slice. The times are simulated.
32 devices in a mesh: sample: 2 (over y), gx: 8 (over z, x), gy: 2 (over core).
Axes of the slice: x: 2, y: 2, z: 4, core: 2. Of those that a mesh axis runs over, the one named last changes fastest.
Arguments:
- body_force: float32 [3, 64, 32, 256], P(None, 'sample', 'gx', 'gy'), parts along dimension 1, may hold values from -36 to 36
- modulus: float32 [64, 32, 256], P('sample', 'gx', 'gy'), parts along dimension 0, may hold values from 0.12 to 8.2
Outputs:
- solution_field: float32 [3, 64, 32, 256], P(None, 'sample', 'gx', 'gy'), parts along dimension 1
- stress: float32 [6, 64, 32, 256], P(None, 'sample', 'gx', 'gy'), parts along dimension 1
There are 2 independent parts, one for each index of `sample`. A program takes and returns all parts, laid end to end along the dimension named above; each array names one. Nothing has to cross between parts.
All inputs are finite; a program needn't handle non-finite values.
Results may differ from a plain program's by a relative error of at most 0.0039.
Values sent between devices are 32-bit elements; how exact they have to be, the bound alone decides.
A program may use at most 64 MiB of HBM per device.

v0:
```python
import math

import jax
import jax.numpy as jnp
import numpy as np
from jax import lax
from jax.sharding import PartitionSpec as P

ITERS = 2


def shifted(value, axis, by):
    size = lax.axis_size(axis)
    pairs = [(i, i + by) for i in range(size) if 0 <= i + by < size]
    return lax.ppermute(value, axis, pairs)


def corner_list():
    return [(off_z, off_x, off_y) for off_z in (0, 1) for off_x in (0, 1) for off_y in (0, 1)]


def strain_matrix(point):
    corners = corner_list()
    grads = np.zeros((3, 8))
    for corner, offsets in enumerate(corners):
        for axis in range(3):
            value = 1.0 if offsets[axis] else -1.0
            for other in range(3):
                if other != axis:
                    value = value * (point[other] if offsets[other] else 1.0 - point[other])
            grads[axis, corner] = value
    strain = np.zeros((6, 24))
    for corner in range(8):
        for axis in range(3):
            strain[axis, axis * 8 + corner] = grads[axis, corner]
        strain[3, 0 * 8 + corner] = grads[1, corner]
        strain[3, 1 * 8 + corner] = grads[0, corner]
        strain[4, 1 * 8 + corner] = grads[2, corner]
        strain[4, 2 * 8 + corner] = grads[1, corner]
        strain[5, 0 * 8 + corner] = grads[2, corner]
        strain[5, 2 * 8 + corner] = grads[0, corner]
    return strain


def tables():
    poisson = 0.3
    lame_first = poisson / ((1.0 + poisson) * (1.0 - 2.0 * poisson))
    shear_mod = 1.0 / (2.0 * (1.0 + poisson))
    elastic = np.zeros((6, 6))
    elastic[:3, :3] = lame_first
    for axis in range(3):
        elastic[axis, axis] += 2.0 * shear_mod
        elastic[axis + 3, axis + 3] = shear_mod
    gauss_pts = [0.5 - 0.5 / math.sqrt(3.0), 0.5 + 0.5 / math.sqrt(3.0)]
    stiffness = np.zeros((24, 24))
    for first in gauss_pts:
        for second in gauss_pts:
            for third in gauss_pts:
                strain = strain_matrix((first, second, third))
                stiffness += strain.T @ elastic @ strain / 8.0
    stress_map = elastic @ strain_matrix((0.5, 0.5, 0.5))
    return (jnp.asarray(stiffness, jnp.float32), jnp.asarray(stress_map, jnp.float32))


def element_values(padded, modulus, matrix):
    z_cells, x_cells, y_cells = modulus.shape
    pieces = [
        padded[channel, off_z : off_z + z_cells, off_x : off_x + x_cells, off_y : off_y + y_cells]
        for channel in range(3)
        for off_z, off_x, off_y in corner_list()
    ]
    stacked = jnp.stack(pieces)
    result = jnp.einsum("pq,qzxy->pzxy", matrix, stacked, precision=lax.Precision.HIGHEST)
    return result * modulus


def spread(values, per_corner):
    summed = None
    for corner, (off_z, off_x, off_y) in enumerate(corner_list()):
        corner_part = values[corner::8] if per_corner else values
        placed = jnp.pad(
            corner_part, ((0, 0), (off_z, 1 - off_z), (off_x, 1 - off_x), (off_y, 1 - off_y))
        )
        summed = placed if summed is None else summed + placed
    return summed


def lower_ghost(field_in):
    below = shifted(field_in[:, :, -1:, :], "gx", 1)
    extended = jnp.concatenate([below, field_in], axis=2)
    beside = shifted(extended[:, :, :, -1:], "gy", 1)
    extended = jnp.concatenate([beside, extended], axis=3)
    return jnp.pad(extended, ((0, 0), (1, 0), (0, 0), (0, 0)))


def fold_back(summed):
    arrived = shifted(summed[:, :, :, :1], "gy", -1)
    summed = jnp.concatenate([summed[:, :, :, 1:-1], summed[:, :, :, -1:] + arrived], axis=3)
    arrived = shifted(summed[:, :, :1, :], "gx", -1)
    summed = jnp.concatenate([summed[:, :, 1:-1, :], summed[:, :, -1:, :] + arrived], axis=2)
    return summed[:, 1:]


def local_factor(cells, offset, total):
    nodes = offset + jnp.arange(cells, dtype=jnp.int32) + 1
    return jnp.where(nodes < total, jnp.float32(2.0), jnp.float32(1.0))


def residual_norm(current):
    return lax.psum(jnp.sum(current * current), ("gx", "gy"))


def per_device(body_force, modulus):
    stiffness, stress_map = tables()
    z_cells, x_cells, y_cells = modulus.shape

    def assemble(field_in, matrix, per_corner):
        padded = lower_ghost(field_in)
        return fold_back(spread(element_values(padded, modulus, matrix), per_corner))

    solution_field = jnp.zeros_like(body_force)
    residual = body_force
    direction = body_force
    norm_now = residual_norm(residual)
    for iteration in range(ITERS):
        image_vec = assemble(direction, stiffness, True)
        step_len = norm_now / lax.psum(jnp.sum(direction * image_vec), ("gx", "gy"))
        solution_field = solution_field + step_len * direction
        residual = residual - step_len * image_vec
        norm_next = residual_norm(residual)
        direction = residual + norm_next / norm_now * direction
        norm_now = norm_next
    summed = assemble(solution_field, stress_map, False)
    x_offset = lax.axis_index("gx") * x_cells
    y_offset = lax.axis_index("gy") * y_cells
    counts = (
        local_factor(z_cells, 0, z_cells)[:, None, None]
        * local_factor(x_cells, x_offset, x_cells * lax.axis_size("gx"))[None, :, None]
        * local_factor(y_cells, y_offset, y_cells * lax.axis_size("gy"))[None, None, :]
    )
    stress = summed / counts
    return (solution_field, stress)


def solution(mesh):
    return jax.shard_map(
        per_device,
        mesh=mesh,
        in_specs=(P(None, "sample", "gx", "gy"), P("sample", "gx", "gy")),
        out_specs=(P(None, "sample", "gx", "gy"), P(None, "sample", "gx", "gy")),
        check_vma=False,
    )
```

profile of v0, /device:TPU:0, one launch (start us, length us, event | category | flops | bytes accessed | tf_op | source)
XLA Modules:
  0.0 243.6 jit_solution(11771306178316561756)
XLA Ops:
  0.6 1.0 slice.523
  1.7 4.8 %collective-permute-start = (f32[3,32,1,128]{3,0,2,1:T(4,128)S(1)}, f32[3,32,1,128]{3,0,2,1:T(4,128)S(1)}, u32[]{:S(2)}, u32[]{:S(2)}) collective-permute-start(f32[3,32,1,128]{3,0,2,1:T(4,128)S(1)} %copy.37), channel_id=1, source_target_pairs={{0,2},{2,4},{4,6},{6,8},{8,10},{10,12},{12,14},{1,3},{3,5},{5,7},{... | collective-permute-start | bytes 147464 | tf_op jit(solution)/shard_map/ppermute | solution.py:15
  6.6 0.9 fusion.29
  7.5 1.0 collective-permute-done
  8.5 1.1 copy_dynamic-update-slice_fusion
  9.8 1.3 collective-permute-start.1
  13.8 1.0 fusion.20
  14.8 2.5 %stack.9 = f32[24,32,4,128]{3,0,2,1:T(8,128)S(1)} concatenate(f32[1,32,4,128]{3,0,2,1:T(1,128)S(1)} %get-tuple-element.61, f32[1,32,4,128]{3,0,2,1:T(1,128)S(1)} %get-tuple-element.51, f32[1,32,4,128]{3,0,2,1:T(1,128)S(1)} %get-tuple-element.52, f32[1,32,4,128]{3,0,2,1:T(1,128)S(1)} %get-tuple-element.53, f32[1,32,4,128]{3,0,2,1:T(1,128)S(1)} %get-tuple-element.45, ...), dimensions={0} | concatenate | bytes 3145728 | tf_op jit(solution)/shard_map/stack | solution.py:72
  17.3 1.4 multiply_bitcast_fusion.1
  18.8 0.9 slice.434
  19.6 0.9 slice.435
  20.5 0.9 slice.436
  21.4 0.9 slice.437
  22.3 0.9 slice.438
  24.0 9.7 %slice.440 = f32[3,32,4,128]{3,0,2,1:T(4,128)} slice(f32[24,32,4,128]{3,0,2,1:T(8,128)S(1)} %multiply_bitcast_fusion.1), slice={[6:24:8], [0:32:1], [0:4:1], [0:128:1]} | slice | bytes 393216 | tf_op jit(solution)/shard_map/slice | solution.py:80
  33.7 9.8 %slice.441 = f32[3,32,4,128]{3,0,2,1:T(4,128)} slice(f32[24,32,4,128]{3,0,2,1:T(8,128)S(1)} %multiply_bitcast_fusion.1), slice={[7:24:8], [0:32:1], [0:4:1], [0:128:1]} | slice | bytes 393216 | tf_op jit(solution)/shard_map/slice | solution.py:80
  43.5 2.2 pad_add_fusion.2
  45.7 1.3 collective-permute-start.2
  47.3 2.0 collective-permute-done.2
  49.5 1.3 collective-permute-start.3
  51.0 5.2 %collective-permute-done.3 = f32[3,33,1,128]{3,0,2,1:T(4,128)S(1)} collective-permute-done((f32[3,33,1,128]{3,0,2,1:T(4,128)S(1)}, f32[3,33,1,128]{3,0,2,1:T(4,128)S(1)}, u32[]{:S(2)}, u32[]{:S(2)}) %collective-permute-start.3) | collective-permute-done | bytes 50720 | tf_op jit(solution)/shard_map/ppermute | solution.py:15
  57.1 32.9 %all-reduce.27 = (f32[]{:T(128)}, f32[]{:T(128)}) all-reduce(f32[]{:T(128)} %multiply_reduce_fusion.2, f32[]{:T(128)} %multiply_reduce_fusion.1), channel_id=1, replica_groups=mesh['sample'=2,'gx'=8,'gy'=2] {'gx','gy'}, use_global_device_ids=true, to_apply=%region_1.0 | all-reduce | flops 2 | bytes 16 | tf_op jit(solution)/shard_map/psum | solution.py:110
  92.1 30.2 %psum.30 = f32[]{:T(128)} all-reduce(f32[]{:T(128)} %multiply_reduce_fusion), channel_id=1, replica_groups=mesh['sample'=2,'gx'=8,'gy'=2] {'gx','gy'}, use_global_device_ids=true, to_apply=%region_5.6 | all-reduce | flops 1 | bytes 8 | tf_op jit(solution)/shard_map/psum | solution.py:110
  123.8 1.3 collective-permute-start.4
  125.1 1.9 collective-permute-done.4
  127.2 1.5 collective-permute-start.5
  130.1 0.9 fusion.27
  131.5 4.6 %stack.10 = f32[24,32,4,128]{3,0,2,1:T(8,128)} concatenate(f32[1,32,4,128]{3,0,2,1:T(1,128)S(1)} %get-tuple-element.43, f32[1,32,4,128]{3,0,2,1:T(1,128)S(1)} %get-tuple-element.27, f32[1,32,4,128]{3,0,2,1:T(1,128)S(1)} %get-tuple-element.28, f32[1,32,4,128]{3,0,2,1:T(1,128)S(1)} %get-tuple-element.29, f32[1,32,4,128]{3,0,2,1:T(1,128)S(1)} %get-tuple-element.42, ...), dimensions={0} | concatenate | bytes 3145728 | tf_op jit(solution)/shard_map/stack | solution.py:72
  136.0 2.8 %multiply_bitcast_fusion = f32[24,32,4,128]{3,0,2,1:T(8,128)S(1)} fusion(f32[24,32,4,128]{3,0,2,1:T(8,128)} %stack.10, f32[24,24,1,1]{1,0,3,2:T(8,128)S(1)} %copy-done.2, f32[32,4,128]{2,1,0:T(4,128)S(1)} %copy-done.1), kind=kOutput, calls=%fused_computation | convolution fusion | flops 113639424 | bytes 3213568 | tf_op jit(solution)/shard_map/pq,qzxy->pzxy/dot_general | solution.py:73
  143.2 9.7 %slice.480 = f32[3,32,4,128]{3,0,2,1:T(4,128)} slice(f32[24,32,4,128]{3,0,2,1:T(8,128)S(1)} %multiply_bitcast_fusion), slice={[5:24:8], [0:32:1], [0:4:1], [0:128:1]} | slice | bytes 393216 | tf_op jit(solution)/shard_map/slice | solution.py:80
  153.0 9.7 %slice.481 = f32[3,32,4,128]{3,0,2,1:T(4,128)} slice(f32[24,32,4,128]{3,0,2,1:T(8,128)S(1)} %multiply_bitcast_fusion), slice={[6:24:8], [0:32:1], [0:4:1], [0:128:1]} | slice | bytes 393216 | tf_op jit(solution)/shard_map/slice | solution.py:80
  162.7 9.8 %slice.482 = f32[3,32,4,128]{3,0,2,1:T(4,128)} slice(f32[24,32,4,128]{3,0,2,1:T(8,128)S(1)} %multiply_bitcast_fusion), slice={[7:24:8], [0:32:1], [0:4:1], [0:128:1]} | slice | bytes 393216 | tf_op jit(solution)/shard_map/slice | solution.py:80
  172.5 2.2 pad_add_fusion.1
  174.8 1.3 collective-permute-start.6
  176.4 1.9 collective-permute-done.6
  178.5 1.3 collective-permute-start.7
  180.0 5.2 %collective-permute-done.7 = f32[3,33,1,128]{3,0,2,1:T(4,128)S(1)} collective-permute-done((f32[3,33,1,128]{3,0,2,1:T(4,128)S(1)}, f32[3,33,1,128]{3,0,2,1:T(4,128)S(1)}, u32[]{:S(2)}, u32[]{:S(2)}) %collective-permute-start.7) | collective-permute-done | bytes 50720 | tf_op jit(solution)/shard_map/ppermute | solution.py:15
  186.1 30.1 %psum.31 = f32[]{:T(128)} all-reduce(f32[]{:T(128)} %fusion.6), channel_id=1, replica_groups=mesh['sample'=2,'gx'=8,'gy'=2] {'gx','gy'}, use_global_device_ids=true, to_apply=%region_7.8 | all-reduce | flops 1 | bytes 8 | tf_op jit(solution)/shard_map/psum | solution.py:127
  217.7 1.3 collective-permute-start.8
  219.0 1.9 collective-permute-done.8
  221.1 1.5 collective-permute-start.9
  224.1 0.9 fusion.25
  225.4 2.5 %stack.11 = f32[24,32,4,128]{3,0,2,1:T(8,128)S(1)} concatenate(f32[1,32,4,128]{3,0,2,1:T(1,128)S(1)} %get-tuple-element.25, f32[1,32,4,128]{3,0,2,1:T(1,128)S(1)} %get-tuple-element.9, f32[1,32,4,128]{3,0,2,1:T(1,128)S(1)} %get-tuple-element.10, f32[1,32,4,128]{3,0,2,1:T(1,128)S(1)} %get-tuple-element.11, f32[1,32,4,128]{3,0,2,1:T(1,128)S(1)} %get-tuple-element.24, ...), dimensions={0} | concatenate | bytes 3145728 | tf_op jit(solution)/shard_map/stack | solution.py:72
  227.9 0.9 fusion
  228.9 1.1 pad_add_fusion
  230.4 1.3 collective-permute-start.10
  234.1 1.3 collective-permute-start.11
  235.6 7.0 %collective-permute-done.11 = f32[6,33,1,128]{3,0,2,1:T(8,128)S(1)} collective-permute-done((f32[6,33,1,128]{3,0,2,1:T(8,128)S(1)}, f32[6,33,1,128]{3,0,2,1:T(8,128)S(1)}, u32[]{:S(2)}, u32[]{:S(2)}) %collective-permute-start.11) | collective-permute-done | bytes 101408 | tf_op jit(solution)/shard_map/ppermute | solution.py:15
  (68 shorter events, 20.6 us)
Async XLA Ops:
  0.6 10.5 %copy-start = (f32[3,32,4,128]{3,2,1,0:T(4,128)S(1)}, f32[3,32,4,128]{3,2,1,0:T(4,128)}, u32[]{:S(2)}) copy-start(f32[3,32,4,128]{3,2,1,0:T(4,128)} %param.4) | copy-start | bytes 589828
  1.7 6.7 %collective-permute-start = (f32[3,32,1,128]{3,0,2,1:T(4,128)S(1)}, f32[3,32,1,128]{3,0,2,1:T(4,128)S(1)}, u32[]{:S(2)}, u32[]{:S(2)}) collective-permute-start(f32[3,32,1,128]{3,0,2,1:T(4,128)S(1)} %copy.37), channel_id=1, source_target_pairs={{0,2},{2,4},{4,6},{6,8},{8,10},{10,12},{12,14},{1,3},{3,5},{5,7},{... | collective-permute-start | bytes 147464 | tf_op jit(solution)/shard_map/ppermute | solution.py:15
  9.8 2.5 %collective-permute-start.1 = (f32[3,32,5,1]{3,0,2,1:T(4,128)S(1)}, f32[3,32,5,1]{3,0,2,1:T(4,128)S(1)}, u32[]{:S(2)}, u32[]{:S(2)}) collective-permute-start(f32[3,32,5,1]{3,0,2,1:T(4,128)S(1)} %slice.524), channel_id=1, source_target_pairs={{0,1},{2,3},{4,5},{6,7},{8,9},{10,11},{12,13},{14,15},{16,17},{18,... | collective-permute-start | bytes 5768 | tf_op jit(solution)/shard_map/ppermute | solution.py:15
  14.8 2.5 %copy-start.1 = (f32[32,4,128]{2,1,0:T(4,128)S(1)}, f32[32,4,128]{2,1,0:T(4,128)}, u32[]{:S(2)}) copy-start(f32[32,4,128]{2,1,0:T(4,128)} %param.5) | copy-start | bytes 196612
  14.8 2.5 %copy-start.2 = (f32[24,24,1,1]{1,0,3,2:T(8,128)S(1)}, f32[24,24,1,1]{1,0,3,2:T(8,128)}, u32[]{:S(2)}) copy-start(f32[24,24,1,1]{1,0,3,2:T(8,128)} %constant.91) | copy-start | bytes 6916
  45.7 3.5 %collective-permute-start.2 = (f32[3,33,5,1]{3,0,2,1:T(4,128)S(1)}, f32[3,33,5,1]{3,0,2,1:T(4,128)S(1)}, u32[]{:S(2)}, u32[]{:S(2)}) collective-permute-start(f32[3,33,5,1]{3,0,2,1:T(4,128)S(1)} %slice.542), channel_id=1, source_target_pairs={{1,0},{3,2},{5,4},{7,6},{9,8},{11,10},{13,12},{15,14},{17,16},{19,... | collective-permute-start | bytes 5948 | tf_op jit(solution)/shard_map/ppermute | solution.py:15
  49.5 6.7 %collective-permute-start.3 = (f32[3,33,1,128]{3,0,2,1:T(4,128)S(1)}, f32[3,33,1,128]{3,0,2,1:T(4,128)S(1)}, u32[]{:S(2)}, u32[]{:S(2)}) collective-permute-start(f32[3,33,1,128]{3,0,2,1:T(4,128)S(1)} %pad_maximum_fusion.6), channel_id=1, source_target_pairs={{2,0},{4,2},{6,4},{8,6},{10,8},{12,10},{14,12},{3,1},{5,3},{7,5},{... | collective-permute-start | bytes 152072 | tf_op jit(solution)/shard_map/ppermute | solution.py:15
  123.8 3.2 %collective-permute-start.4 = (f32[3,32,1,128]{3,0,2,1:T(4,128)S(1)}, f32[3,32,1,128]{3,0,2,1:T(4,128)S(1)}, u32[]{:S(2)}, u32[]{:S(2)}) collective-permute-start(f32[3,32,1,128]{3,0,2,1:T(4,128)S(1)} %slice.547), channel_id=1, source_target_pairs={{0,2},{2,4},{4,6},{6,8},{8,10},{10,12},{12,14},{1,3},{3,5},{5,7},{... | collective-permute-start | bytes 147464 | tf_op jit(solution)/shard_map/ppermute | solution.py:15
  127.2 2.5 %collective-permute-start.5 = (f32[3,32,5,1]{3,0,2,1:T(4,128)S(1)}, f32[3,32,5,1]{3,0,2,1:T(4,128)S(1)}, u32[]{:S(2)}, u32[]{:S(2)}) collective-permute-start(f32[3,32,5,1]{3,0,2,1:T(4,128)S(1)} %fusion.4), channel_id=1, source_target_pairs={{0,1},{2,3},{4,5},{6,7},{8,9},{10,11},{12,13},{14,15},{16,17},{18,... | collective-permute-start | bytes 5768 | tf_op jit(solution)/shard_map/ppermute | solution.py:15
  174.8 3.5 %collective-permute-start.6 = (f32[3,33,5,1]{3,0,2,1:T(4,128)S(1)}, f32[3,33,5,1]{3,0,2,1:T(4,128)S(1)}, u32[]{:S(2)}, u32[]{:S(2)}) collective-permute-start(f32[3,33,5,1]{3,0,2,1:T(4,128)S(1)} %slice.565), channel_id=1, source_target_pairs={{1,0},{3,2},{5,4},{7,6},{9,8},{11,10},{13,12},{15,14},{17,16},{19,... | collective-permute-start | bytes 5948 | tf_op jit(solution)/shard_map/ppermute | solution.py:15
  178.5 6.7 %collective-permute-start.7 = (f32[3,33,1,128]{3,0,2,1:T(4,128)S(1)}, f32[3,33,1,128]{3,0,2,1:T(4,128)S(1)}, u32[]{:S(2)}, u32[]{:S(2)}) collective-permute-start(f32[3,33,1,128]{3,0,2,1:T(4,128)S(1)} %pad_maximum_fusion.5), channel_id=1, source_target_pairs={{2,0},{4,2},{6,4},{8,6},{10,8},{12,10},{14,12},{3,1},{5,3},{7,5},{... | collective-permute-start | bytes 152072 | tf_op jit(solution)/shard_map/ppermute | solution.py:15
  217.7 3.2 %collective-permute-start.8 = (f32[3,32,1,128]{3,0,2,1:T(4,128)S(1)}, f32[3,32,1,128]{3,0,2,1:T(4,128)S(1)}, u32[]{:S(2)}, u32[]{:S(2)}) collective-permute-start(f32[3,32,1,128]{3,0,2,1:T(4,128)S(1)} %slice.570), channel_id=1, source_target_pairs={{0,2},{2,4},{4,6},{6,8},{8,10},{10,12},{12,14},{1,3},{3,5},{5,7},{... | collective-permute-start | bytes 147464 | tf_op jit(solution)/shard_map/ppermute | solution.py:15
  221.1 2.5 %collective-permute-start.9 = (f32[3,32,5,1]{3,0,2,1:T(4,128)S(1)}, f32[3,32,5,1]{3,0,2,1:T(4,128)S(1)}, u32[]{:S(2)}, u32[]{:S(2)}) collective-permute-start(f32[3,32,5,1]{3,0,2,1:T(4,128)S(1)} %fusion.3), channel_id=1, source_target_pairs={{0,1},{2,3},{4,5},{6,7},{8,9},{10,11},{12,13},{14,15},{16,17},{18,... | collective-permute-start | bytes 5768 | tf_op jit(solution)/shard_map/ppermute | solution.py:15
  225.4 2.5 %copy-start.3 = (f32[6,24,1,1]{1,0,3,2:T(8,128)S(1)}, f32[6,24,1,1]{1,0,3,2:T(8,128)}, u32[]{:S(2)}) copy-start(f32[6,24,1,1]{1,0,3,2:T(8,128)} %constant.92) | copy-start | bytes 1732
  230.4 3.1 %collective-permute-start.10 = (f32[6,33,5,1]{1,3,2,0:T(1,128)S(1)}, f32[6,33,5,1]{1,3,2,0:T(1,128)S(1)}, u32[]{:S(2)}, u32[]{:S(2)}) collective-permute-start(f32[6,33,5,1]{1,3,2,0:T(1,128)S(1)} %copy.26), channel_id=1, source_target_pairs={{1,0},{3,2},{5,4},{7,6},{9,8},{11,10},{13,12},{15,14},{17,16},{19,... | collective-permute-start | bytes 11888 | tf_op jit(solution)/shard_map/ppermute | solution.py:15
  234.1 8.4 %collective-permute-start.11 = (f32[6,33,1,128]{3,0,2,1:T(8,128)S(1)}, f32[6,33,1,128]{3,0,2,1:T(8,128)S(1)}, u32[]{:S(2)}, u32[]{:S(2)}) collective-permute-start(f32[6,33,1,128]{3,0,2,1:T(8,128)S(1)} %pad_maximum_fusion.4), channel_id=1, source_target_pairs={{2,0},{4,2},{6,4},{8,6},{10,8},{12,10},{14,12},{3,1},{5,3},{7,5},{... | collective-permute-start | bytes 304136 | tf_op jit(solution)/shard_map/ppermute | solution.py:15
where the time goes:
time: 244 us
  blocking collectives  93.2 us (38%)
  local copies, waits for them, and re-layouts  78 us (32%)
  waiting for transfers between devices  28.7 us (12%)
  starting transfers between devices  19.5 us (8%)
  other arithmetic  13.8 us (6%)
  matrix products  5.21 us (2%)
  between operations  5.18 us (2%)
    psum x2, blocking collectives, residual_norm(): return lax.psum(jnp.sum(current * current), ('gx', 'gy'))  63.1 us
    slice x16, local copies, waits for them, and re-layouts, spread(): corner_part = values[corner::8] if per_corner else values  58.2 us
    psum x1, blocking collectives, per_device(): step_len = norm_now / lax.psum(jnp.sum(direction * image_vec), ('gx', 'gy'))  30.1 us
    ppermute x12, waiting for transfers between devices, shifted(): return lax.ppermute(value, axis, pairs)  28.7 us
    ppermute x12, starting transfers between devices, shifted(): return lax.ppermute(value, axis, pairs)  19.5 us
    another operation x3, local copies, waits for them, and re-layouts, element_values(): stacked = jnp.stack(pieces)  9.54 us
    add x3, other arithmetic, spread(): summed = placed if summed is None else summed + placed  5.56 us
    dot_general x3, matrix products, element_values(): jnp.einsum('pq,qzxy->pzxy', matrix, stacked, precision=lax.Precision.HIGH...  5.21 us
  transfers between devices with their start and end apart: 12, of which 12 were waited for; matrix products, arithmetic and copies ran while one was open for 2% of the time, Pallas kernels for 0%

commit v1 on v0

v1 whole, which is shorter than its diff:
```python
import functools
import math

import jax
import jax.numpy as jnp
import numpy as np
from jax import lax
from jax.experimental import pallas as pl
from jax.experimental.pallas import tpu as pltpu
from jax.sharding import PartitionSpec as P

MESH = pl.DeviceIdType.MESH


def corner_list():
    return [(off_z, off_x, off_y) for off_z in (0, 1) for off_x in (0, 1) for off_y in (0, 1)]


def strain_matrix(point):
    corners = corner_list()
    grads = np.zeros((3, 8))
    for corner, offsets in enumerate(corners):
        for axis in range(3):
            value = 1.0 if offsets[axis] else -1.0
            for other in range(3):
                if other != axis:
                    value = value * (point[other] if offsets[other] else 1.0 - point[other])
            grads[axis, corner] = value
    strain = np.zeros((6, 24))
    for corner in range(8):
        for axis in range(3):
            strain[axis, axis * 8 + corner] = grads[axis, corner]
        strain[3, 0 * 8 + corner] = grads[1, corner]
        strain[3, 1 * 8 + corner] = grads[0, corner]
        strain[4, 1 * 8 + corner] = grads[2, corner]
        strain[4, 2 * 8 + corner] = grads[1, corner]
        strain[5, 0 * 8 + corner] = grads[2, corner]
        strain[5, 2 * 8 + corner] = grads[0, corner]
    return strain


def modal_tables():
    poisson = 0.3
    lame_first = poisson / ((1.0 + poisson) * (1.0 - 2.0 * poisson))
    shear_mod = 1.0 / (2.0 * (1.0 + poisson))
    elastic = np.zeros((6, 6))
    elastic[:3, :3] = lame_first
    for axis in range(3):
        elastic[axis, axis] += 2.0 * shear_mod
        elastic[axis + 3, axis + 3] = shear_mod
    gauss_pts = [0.5 - 0.5 / math.sqrt(3.0), 0.5 + 0.5 / math.sqrt(3.0)]
    stiffness = np.zeros((24, 24))
    for first in gauss_pts:
        for second in gauss_pts:
            for third in gauss_pts:
                strain = strain_matrix((first, second, third))
                stiffness += strain.T @ elastic @ strain / 8.0
    stress_map = elastic @ strain_matrix((0.5, 0.5, 0.5))
    pair = np.array([[1.0, 1.0], [-1.0, 1.0]])
    modes = np.kron(np.eye(3), np.kron(pair, np.kron(pair, pair)))
    stiffness = modes @ stiffness @ modes.T / 64.0
    stress_map = stress_map @ modes.T / 8.0

    def rows_of(matrix):
        out = []
        for row in matrix:
            terms = [(q // 8, (q % 8) // 4, (q % 4) // 2, q % 2, float(v)) for q, v in enumerate(row) if abs(v) > 1e-9]
            out.append(terms)
        return out

    return rows_of(stiffness), rows_of(stress_map)


STIFF, STRESS = modal_tables()
B_RIGHT, P_RIGHT, S_RIGHT, D_RIGHT, B_LEFT, E_LEFT, Q_LEFT, S_LEFT, D_LEFT, S_OTHER = range(10)


def combine(terms, fields):
    total = None
    for c, a, b, d, value in terms:
        part = fields[c][a, b, d] * np.float32(value)
        total = part if total is None else total + part
    return total


def kernel(n_gx, n_gy, f_hbm, e_hbm, x_out, s_out,
           f_in, e_in, b_ref, e_ref, bl, pp, br, er, qq, p_out, q_out,
           msg, st_same, st_other, w_ref, ws_ref, bs_ref, sb_ref, sw_ref, ssb_ref, ssw_ref,
           red, slots, in_sem, send_sem, recv_sem, red_send, red_recv):
    gx, gy = lax.axis_index("gx"), lax.axis_index("gy")
    rows = e_hbm.shape[0]
    planes, depth, width = b_ref.shape[0], b_ref.shape[2], b_ref.shape[3]
    has_left, has_right = gx > 0, gx < n_gx - 1
    other = 1 - gy
    n = n_gx * n_gy
    me = gx * n_gy + gy

    load_f = pltpu.make_async_copy(f_hbm, f_in, in_sem.at[0])
    load_e = pltpu.make_async_copy(e_hbm, e_in, in_sem.at[1])
    load_f.start()
    load_e.start()

    barrier = pltpu.get_barrier_semaphore()

    def member(k):
        target = lax.rem(me + k, n)
        return {"gx": target // n_gy, "gy": lax.rem(target, n_gy)}

    def each_member(body):
        if n <= 32:
            for k in range(1, n):
                body(k)
        else:
            lax.fori_loop(1, n, lambda k, carry: (body(k), carry)[1], 0)

    each_member(lambda k: pl.semaphore_signal(barrier, inc=1, device_id=member(k), device_id_type=MESH))

    shape = (depth, width)
    lane = lax.broadcasted_iota(jnp.int32, shape, 1)
    row = lax.broadcasted_iota(jnp.int32, shape, 0)
    zero = jnp.zeros(shape, jnp.float32)
    first_row, last_row = row == 0, row == depth - 1
    first_lane, last_lane = lane == 0, lane == width - 1

    @pl.when(gx == 0)
    def _():
        bl[...] = jnp.zeros_like(bl)
        pp[...] = jnp.zeros_like(pp)
        st_same[0] = zero
        st_other[0] = zero

    @pl.when(gx == n_gx - 1)
    def _():
        br[...] = jnp.zeros_like(br)
        er[...] = jnp.zeros_like(er)
        qq[...] = jnp.zeros_like(qq)
        st_same[1] = zero
        st_other[3] = zero

    def remote(src, dst, which, x, y):
        return pltpu.make_async_remote_copy(
            src_ref=src, dst_ref=dst, send_sem=send_sem.at[which], recv_sem=recv_sem.at[which],
            device_id={"gx": x, "gy": y}, device_id_type=MESH)

    right, left = lax.rem(gx + 1, n_gx), lax.rem(gx + n_gx - 1, n_gx)
    to_right = {
        B_RIGHT: remote(b_ref.at[planes - 1], bl, B_RIGHT, right, gy),
        P_RIGHT: remote(p_out, pp, P_RIGHT, right, gy),
        S_RIGHT: remote(msg.at[1], st_same.at[0], S_RIGHT, right, gy),
        D_RIGHT: remote(msg.at[1], st_other.at[0], D_RIGHT, right, other),
    }
    to_left = {
        B_LEFT: remote(b_ref.at[0], br, B_LEFT, left, gy),
        E_LEFT: remote(e_ref.at[0], er, E_LEFT, left, gy),
        Q_LEFT: remote(q_out, qq, Q_LEFT, left, gy),
        S_LEFT: remote(msg.at[0], st_same.at[1], S_LEFT, left, gy),
        D_LEFT: remote(msg.at[0], st_other.at[3], D_LEFT, left, other),
    }
    to_other = remote(msg, st_other.at[pl.ds(1, 2)], S_OTHER, gx, other)

    def start(rights, lefts):
        @pl.when(has_right)
        def _():
            for which in rights:
                to_right[which].start()

        @pl.when(has_left)
        def _():
            for which in lefts:
                to_left[which].start()

    def arrived(rights, lefts):
        @pl.when(has_left)
        def _():
            for which in rights:
                to_right[which].wait_recv()

        @pl.when(has_right)
        def _():
            for which in lefts:
                to_left[which].wait_recv()

    load_f.wait()
    load_e.wait()
    for p in range(planes):
        for c in range(3):
            b_ref[p, c] = f_in[c, pl.ds(p, depth, stride=planes), :]
        e_ref[p] = e_in[pl.ds(p, depth, stride=planes), :]

    pl.semaphore_wait(barrier, n - 1)
    start([B_RIGHT], [B_LEFT, E_LEFT])

    for side in range(2):
        packed = None
        for c in range(4):
            for t in range(2):
                p = 2 * side + t
                value = b_ref[p, c] if c < 3 else e_ref[p]
                turned = pltpu.roll(value, (32 * c + 16 * t + 8) % width, 1)
                packed = turned if packed is None else jnp.where(lane // 16 == 2 * c + t, turned, packed)
        msg[side] = packed
    to_other.start()
    start([S_RIGHT, D_RIGHT], [S_LEFT, D_LEFT])

    def y_below(value, edge):
        value = pltpu.roll(value, 1, 1)
        return jnp.where(first_lane, 0.0, value) if edge else value

    def y_above(value, edge):
        value = pltpu.roll(value, width - 1, 1)
        return jnp.where(last_lane, 0.0, value) if edge else value

    def z_below(value):
        return jnp.where(first_row, 0.0, pltpu.roll(value, 1, 0))

    def z_above(value):
        return jnp.where(last_row, 0.0, pltpu.roll(value, depth - 1, 0))

    def forward(value, edge):
        below = y_below(value, edge)
        out = {}
        for d, part in ((0, value + below), (1, value - below)):
            low = z_below(part)
            out[0, d], out[1, d] = part + low, part - low
        return out

    def pair_up(low, high):
        fields = []
        for c in range(3):
            field = {}
            for key in high[c]:
                a, d = key
                field[a, 0, d] = high[c][key] + low[c][key]
                field[a, 1, d] = high[c][key] - low[c][key]
            fields.append(field)
        return fields

    def forces(fields, scale):
        highs, lows = [], []
        for c in range(3):
            high, low = {}, {}
            for a in range(2):
                for d in range(2):
                    diff = combine(STIFF[c * 8 + 4 * a + 2 + d], fields) * scale
                    terms = STIFF[c * 8 + 4 * a + d]
                    if terms:
                        same = combine(terms, fields) * scale
                        high[a, d], low[a, d] = same + diff, same - diff
                    else:
                        high[a, d], low[a, d] = diff, -diff
            highs.append(high)
            lows.append(low)
        return highs, lows

    def back(modes, edge):
        parts = []
        for d in range(2):
            parts.append(modes[0, d] + modes[1, d] + z_above(modes[0, d] - modes[1, d]))
        return parts[0] + parts[1] + y_above(parts[0] - parts[1], edge)

    def add(first, second):
        return {key: first[key] + second[key] for key in first}

    def energy(fields, scale):
        total = None
        for c in range(3):
            for k in range(1, 8):
                part = combine(STIFF[c * 8 + k], fields) * fields[c][k // 4, (k % 4) // 2, k % 2]
                total = part if total is None else total + part
        return total * scale

    def stresses(fields, scale):
        return [combine(STRESS[r], fields) * scale for r in range(6)]

    def spread(value, edge):
        value = value + z_above(value)
        return value + y_above(value, edge)

    def b_plane(p, c):
        return bl[c] if p < 0 else br[c] if p >= planes else b_ref[p, c]

    def b_modes(p):
        return [forward(b_plane(p, c), True) for c in range(3)]

    m2 = [b_modes(p) for p in range(planes)]
    highs, lows, s_b = {}, {}, {}

    def do_element(p, low, high):
        scale = er[...] if p >= planes else e_ref[p]
        fields = pair_up(low, high)
        highs[p], lows[p] = forces(fields, scale)
        s_b[p] = stresses(fields, scale)

    do_element(planes - 1, m2[planes - 2], m2[planes - 1])
    for c in range(3):
        p_out[c] = back(highs[planes - 1][c], True)
    do_element(1, m2[0], m2[1])
    for c in range(3):
        q_out[c] = back(lows[1][c], True)
    start([P_RIGHT], [Q_LEFT])
    for p in range(2, planes - 1):
        do_element(p, m2[p - 1], m2[p])
    for p in range(1, planes - 1):
        for c in range(3):
            w_ref[p + 1, c] = back(add(highs[p][c], lows[p + 1][c]), True)
        if p > 1:
            pass
    for p in range(1, planes - 1):
        for r in range(6):
            sb_ref[p, r] = spread(s_b[p][r] + s_b[p + 1][r], True)

    to_other.wait_recv()
    arrived([S_RIGHT, D_RIGHT], [S_LEFT, D_LEFT])
    mine = lax.rem(lane, 16) // 8 == gy
    quarters = [
        jnp.where(mine, st_same[0], st_other[0]),
        jnp.where(mine, msg[0], st_other[1]),
        jnp.where(mine, msg[1], st_other[2]),
        jnp.where(mine, st_same[1], st_other[3]),
    ]
    strip = []
    for c in range(4):
        total = None
        for q in range(4):
            turn = (32 * (q - c)) % width
            turned = pltpu.roll(quarters[q], turn, 1) if turn else quarters[q]
            total = turned if total is None else jnp.where(lane // 32 == q, turned, total)
        strip.append(total)
    strip_e = strip[3]

    def strip_fields(values):
        high = [forward(value, False) for value in values]
        low = [{key: pltpu.roll(field[key], 16, 1) for key in field} for field in high]
        return pair_up(low, high)

    def next_slot(value):
        return pltpu.roll(value, width - 16, 1)

    fields = strip_fields(strip[:3])
    strip_high, strip_low = forces(fields, strip_e)
    s_strip = stresses(fields, strip_e)
    clamped = jnp.logical_and(gx == 0, lane < 32)
    strip_w = []
    for c in range(3):
        modes = {key: strip_high[c][key] + next_slot(strip_low[c][key]) for key in strip_high[c]}
        strip_w.append(jnp.where(clamped, 0.0, back(modes, False)))
    for r in range(6):
        ssb_ref[r] = spread(s_strip[r] + next_slot(s_strip[r]), False)

    at_cut = lane == (width - 1) * other

    def mend(value, strip_value, p):
        turn = (-(16 * (p + 2) + 8)) % width
        turned = pltpu.roll(strip_value, turn, 1) if turn else strip_value
        return jnp.where(at_cut, turned, value)

    arrived([B_RIGHT], [B_LEFT, E_LEFT])
    modes_l, modes_r = b_modes(-1), b_modes(planes)
    do_element(0, modes_l, m2[0])
    do_element(planes, m2[planes - 1], modes_r)
    for p in (0, planes - 1):
        for c in range(3):
            w_ref[p + 1, c] = back(add(highs[p][c], lows[p + 1][c]), True)
        for r in range(6):
            sb_ref[p, r] = spread(s_b[p][r] + s_b[p + 1][r], True)
    arrived([P_RIGHT], [Q_LEFT])
    for c in range(3):
        w_ref[0, c] = jnp.where(gx == 0, 0.0, pp[c] + back(lows[0][c], True))
        w_ref[planes + 1, c] = qq[c] + back(highs[planes][c], True)
    for p in range(-1, planes + 1):
        for c in range(3):
            w_ref[p + 1, c] = mend(w_ref[p + 1, c], strip_w[c], p)

    sum_bb, sum_bw, sum_ww, sum_wkw = zero, zero, zero, zero
    for p in range(planes):
        for c in range(3):
            b, w = b_ref[p, c], w_ref[p + 1, c]
            sum_bb = sum_bb + b * b
            sum_bw = sum_bw + b * w
            sum_ww = sum_ww + w * w
    s_w = {}
    low = [forward(w_ref[0, c], True) for c in range(3)]
    for p in range(planes + 1):
        high = [forward(w_ref[p + 1, c], True) for c in range(3)]
        scale = er[...] if p >= planes else e_ref[p]
        fields = pair_up(low, high)
        if p < planes:
            sum_wkw = sum_wkw + energy(fields, scale)
        s_w[p] = stresses(fields, scale)
        low = high
    sum_wkw = jnp.where(jnp.logical_and(first_lane, gy == 1), 0.0, sum_wkw)
    fields = strip_fields(strip_w)
    s_strip = stresses(fields, strip_e)
    counted = jnp.logical_and(lax.rem(lane, 16) == 8, jnp.logical_and(lane >= 32, lane < 32 + 16 * planes))
    counted = jnp.logical_and(counted, gy == 1)
    sum_wkw = sum_wkw + jnp.where(counted, energy(fields, strip_e), 0.0)

    row8 = lax.broadcasted_iota(jnp.int32, (8, width), 0)
    partial = jnp.zeros((8, width), jnp.float32)
    for k, total in enumerate((sum_bb, sum_bw, sum_ww, sum_wkw)):
        partial = jnp.where(row8 == k, jnp.sum(total, axis=0, keepdims=True), partial)
    red[...] = partial

    def send_sum(k):
        pltpu.make_async_remote_copy(
            src_ref=red, dst_ref=slots.at[k - 1], send_sem=red_send, recv_sem=red_recv,
            device_id=member(k), device_id_type=MESH).start()

    each_member(send_sum)

    for r in range(6):
        ssw_ref[r] = spread(s_strip[r] + next_slot(s_strip[r]), False)
    z_share = jnp.where(last_row, 1.0, 0.5)
    yz_share = z_share * jnp.where(jnp.logical_and(last_lane, gy == n_gy - 1), 1.0, 0.5)
    for p in range(planes):
        share = yz_share * 0.5
        if p == planes - 1:
            share = jnp.where(has_right, share, yz_share)
        for r in range(6):
            value = spread(s_w[p][r] + s_w[p + 1][r], True)
            sw_ref[p, r] = mend(value, ssw_ref[r], p) * share
            sb_ref[p, r] = mend(sb_ref[p, r], ssb_ref[r], p) * share

    pltpu.make_async_copy(slots, slots, red_recv).wait()
    total = red[...]
    if n <= 32:
        for k in range(n - 1):
            total = total + slots[k]
    else:
        total = lax.fori_loop(0, n - 1, lambda k, value: value + slots[k], total)
    sums = jnp.broadcast_to(jnp.sum(total, axis=1, keepdims=True), (8, width))
    bb, bw, ww, wkw = (sums[k : k + 1] for k in range(4))
    first_step = bb / bw
    norm = bb - 2.0 * first_step * bw + first_step * first_step * ww
    ratio = norm / bb
    grown = 1.0 + ratio
    curve = grown * grown * bw - 2.0 * grown * first_step * ww + first_step * first_step * wkw
    second_step = norm / curve
    on_b = first_step + second_step * grown
    on_w = -second_step * first_step
    for p in range(planes):
        for c in range(3):
            x_out[c, pl.ds(p, depth, stride=planes), :] = on_b * b_ref[p, c] + on_w * w_ref[p + 1, c]
        for r in range(6):
            s_out[r, pl.ds(p, depth, stride=planes), :] = on_b * sb_ref[p, r] + on_w * sw_ref[p, r]

    to_other.wait_send()
    pltpu.make_async_copy(slots, slots, red_send).wait()

    @pl.when(has_right)
    def _():
        for copy in to_right.values():
            copy.wait_send()

    @pl.when(has_left)
    def _():
        for copy in to_left.values():
            copy.wait_send()


def solution(mesh):
    n_gx, n_gy = mesh.shape["gx"], mesh.shape["gy"]

    def per_device(body_force, modulus):
        depth, planes, width = modulus.shape
        assert n_gy == 2 and planes == 4 and width == 128
        rows = depth * planes
        n = n_gx * n_gy
        plane = (depth, width)
        vmem = lambda *dims: pltpu.VMEM(dims, jnp.float32)
        field, stress = pl.pallas_call(
            functools.partial(kernel, n_gx, n_gy),
            out_shape=(
                jax.ShapeDtypeStruct((3, rows, width), jnp.float32),
                jax.ShapeDtypeStruct((6, rows, width), jnp.float32),
            ),
            in_specs=[pl.BlockSpec(memory_space=pl.ANY)] * 2,
            out_specs=(pl.BlockSpec(memory_space=pltpu.VMEM),) * 2,
            scratch_shapes=[
                vmem(3, rows, width),
                vmem(rows, width),
                vmem(planes, 3, *plane),
                vmem(planes, *plane),
                vmem(3, *plane),
                vmem(3, *plane),
                vmem(3, *plane),
                vmem(*plane),
                vmem(3, *plane),
                vmem(3, *plane),
                vmem(3, *plane),
                vmem(2, *plane),
                vmem(2, *plane),
                vmem(4, *plane),
                vmem(planes + 2, 3, *plane),
                vmem(3, *plane),
                vmem(3, *plane),
                vmem(planes, 6, *plane),
                vmem(planes, 6, *plane),
                vmem(6, *plane),
                vmem(6, *plane),
                vmem(8, width),
                vmem(n - 1, 8, width),
                pltpu.SemaphoreType.DMA((2,)),
                pltpu.SemaphoreType.DMA((10,)),
                pltpu.SemaphoreType.DMA((10,)),
                pltpu.SemaphoreType.DMA,
                pltpu.SemaphoreType.DMA,
            ],
            compiler_params=pltpu.CompilerParams(
                collective_id=0, has_side_effects=True, vmem_limit_bytes=32 * 1024 * 1024
            ),
        )(body_force.reshape(3, rows, width), modulus.reshape(rows, width))
        return (
            field.reshape(3, depth, planes, width),
            stress.reshape(6, depth, planes, width),
        )

    return jax.shard_map(
        per_device,
        mesh=mesh,
        in_specs=(P(None, "sample", "gx", "gy"), P("sample", "gx", "gy")),
        out_specs=(P(None, "sample", "gx", "gy"), P(None, "sample", "gx", "gy")),
        check_vma=False,
    )
```

time: 244 us -> 22.6 us (0.09)
  blocking collectives: 93.2 us -> 0 us
  local copies, waits for them, and re-layouts: 78 us -> 3.18 us
  waiting for transfers between devices: 28.7 us -> 0 us
  starting transfers between devices: 19.5 us -> 0 us
  Pallas kernels: 0 us -> 18.6 us
  other arithmetic: 13.8 us -> 0 us
  matrix products: 5.21 us -> 0 us
  between operations: 5.18 us -> 0.65 us
    psum x3 -> x0, blocking collectives: 93.2 us -> none  [the longest x2 63.1 us: residual_norm(): return lax.psum(jnp.sum(current * current), ('gx', 'gy'))]
    slice x34 -> x0, local copies, waits for them, and re-layouts: 65.4 us -> none  [the longest x16 58.2 us: spread(): corner_part = values[corner::8] if per_corner else values]
    ppermute x12 -> x0, waiting for transfers between devices: 28.7 us -> none  [shifted(): return lax.ppermute(value, axis, pairs)]
    ppermute x12 -> x0, starting transfers between devices: 19.5 us -> none  [shifted(): return lax.ppermute(value, axis, pairs)]
    pallas_call x0 -> x1, Pallas kernels: none -> 18.6 us  [per_device(): pl.pallas_call(functools.partial(kernel, n_gx, n_gy), out_shape=(jax.Shap...]
    another operation x3 -> x0, local copies, waits for them, and re-layouts: 9.54 us -> none  [element_values(): stacked = jnp.stack(pieces)]
    add x11 -> x0, other arithmetic: 6.53 us -> none  [the longest x3 5.56 us: spread(): summed = placed if summed is None else summed + placed]
    dot_general x3 -> x0, matrix products: 5.21 us -> none  [element_values(): jnp.einsum('pq,qzxy->pzxy', matrix, stacked, precision=lax.Precision.HIGH...]
  transfers between devices with their start and end apart: 12 -> 0, of which waited for: 12 -> 0; matrix products, arithmetic and copies ran while one was open for 2% -> 0% of each run, Pallas kernels for 0% -> 0%
where the time goes in v1:
time: 22.6 us; the launch traced here: 22.4 us
  Pallas kernels  18.6 us (82%)
  local copies, waits for them, and re-layouts  3.18 us (14%)
  between operations  0.65 us (3%)
    pallas_call x1, Pallas kernels, per_device(): pl.pallas_call(functools.partial(kernel, n_gx, n_gy), out_shape=(jax.Shap...  18.6 us
    unnamed x6, local copies, waits for them, and re-layouts  3.18 us

profile of v1, /device:TPU:0, one launch (start us, length us, event | category | flops | bytes accessed | tf_op | source)
XLA Modules:
  0.0 22.4 jit_solution(7488015433022303200)
XLA Ops:
  0.6 0.0 copy-start
  0.6 0.9 %copy-done = f32[3,32,4,128]{3,2,1,0:T(4,128)S(1)} copy-done((f32[3,32,4,128]{3,2,1,0:T(4,128)S(1)}, f32[3,32,4,128]{3,2,1,0:T(4,128)}, u32[]{:S(2)}) %copy-start) | copy-done | bytes 196632
  1.6 0.0 copy-start.1
  1.6 0.8 %copy-done.1 = f32[32,4,128]{2,1,0:T(4,128)S(1)} copy-done((f32[32,4,128]{2,1,0:T(4,128)S(1)}, f32[32,4,128]{2,1,0:T(4,128)}, u32[]{:S(2)}) %copy-start.1) | copy-done | bytes 65560
  2.4 18.6 %shard_map.41 = (f32[3,128,128]{2,1,0:T(8,128)S(1)}, f32[6,128,128]{2,1,0:T(8,128)S(1)}) custom-call(f32[3,128,128]{2,1,0:T(8,128)S(1)} %bitcast.6, f32[128,128]{1,0:T(8,128)S(1)} %bitcast.7), custom_call_target="tpu_custom_call" | custom-call | tf_op jit(solution)/shard_map/pallas_call | solution.py:471
  21.0 0.7 %copy.6 = f32[3,32,4,128]{3,2,1,0:T(4,128)} copy(f32[3,32,4,128]{3,2,1,0:T(4,128)S(1)} %bitcast.5) | data formatting | bytes 393216
  21.7 0.7 %copy.7 = f32[6,32,4,128]{3,2,1,0:T(4,128)} copy(f32[6,32,4,128]{3,2,1,0:T(4,128)S(1)} %bitcast.4) | data formatting | bytes 786432
Async XLA Ops:
  0.6 0.9 %copy-start = (f32[3,32,4,128]{3,2,1,0:T(4,128)S(1)}, f32[3,32,4,128]{3,2,1,0:T(4,128)}, u32[]{:S(2)}) copy-start(f32[3,32,4,128]{3,2,1,0:T(4,128)} %param.2) | copy-start | bytes 589828
  1.6 0.8 %copy-start.1 = (f32[32,4,128]{2,1,0:T(4,128)S(1)}, f32[32,4,128]{2,1,0:T(4,128)}, u32[]{:S(2)}) copy-start(f32[32,4,128]{2,1,0:T(4,128)} %param.3) | copy-start | bytes 196612

commit v2 on v1

--- a/solution.py
+++ b/solution.py
@@ -85,7 +85,7 @@
 
 def kernel(n_gx, n_gy, f_hbm, e_hbm, x_out, s_out,
            f_in, e_in, b_ref, e_ref, bl, pp, br, er, qq, p_out, q_out,
-           msg, st_same, st_other, w_ref, ws_ref, bs_ref, sb_ref, sw_ref, ssb_ref, ssw_ref,
+           msg, st_same, st_other, w_ref, sb_ref, sw_ref, ssb_ref, ssw_ref,
            red, slots, in_sem, send_sem, recv_sem, red_send, red_recv):
     gx, gy = lax.axis_index("gx"), lax.axis_index("gy")
     rows = e_hbm.shape[0]
@@ -180,15 +180,19 @@
             for which in lefts:
                 to_left[which].wait_recv()
 
+    def take(p):
+        for c in range(3):
+            b_ref[p, c] = f_in[c, pl.ds(p, depth, stride=planes), :]
+        e_ref[p] = e_in[pl.ds(p, depth, stride=planes), :]
+
     load_f.wait()
     load_e.wait()
-    for p in range(planes):
-        for c in range(3):
-            b_ref[p, c] = f_in[c, pl.ds(p, depth, stride=planes), :]
-        e_ref[p] = e_in[pl.ds(p, depth, stride=planes), :]
-
+    take(planes - 1)
+    take(0)
     pl.semaphore_wait(barrier, n - 1)
     start([B_RIGHT], [B_LEFT, E_LEFT])
+    for p in range(1, planes - 1):
+        take(p)
 
     for side in range(2):
         packed = None
@@ -300,14 +304,13 @@
     start([P_RIGHT], [Q_LEFT])
     for p in range(2, planes - 1):
         do_element(p, m2[p - 1], m2[p])
+
+    def raw_w(p):
+        for c in range(3):
+            w_ref[p + 1, c] = back(add(highs[p][c], lows[p + 1][c]), True)
+
     for p in range(1, planes - 1):
-        for c in range(3):
-            w_ref[p + 1, c] = back(add(highs[p][c], lows[p + 1][c]), True)
-        if p > 1:
-            pass
-    for p in range(1, planes - 1):
-        for r in range(6):
-            sb_ref[p, r] = spread(s_b[p][r] + s_b[p + 1][r], True)
+        raw_w(p)
 
     to_other.wait_recv()
     arrived([S_RIGHT, D_RIGHT], [S_LEFT, D_LEFT])
@@ -354,50 +357,86 @@
         turned = pltpu.roll(strip_value, turn, 1) if turn else strip_value
         return jnp.where(at_cut, turned, value)
 
-    arrived([B_RIGHT], [B_LEFT, E_LEFT])
-    modes_l, modes_r = b_modes(-1), b_modes(planes)
-    do_element(0, modes_l, m2[0])
-    do_element(planes, m2[planes - 1], modes_r)
-    for p in (0, planes - 1):
-        for c in range(3):
-            w_ref[p + 1, c] = back(add(highs[p][c], lows[p + 1][c]), True)
+    z_share = jnp.where(last_row, 1.0, 0.5)
+    yz_share = z_share * jnp.where(jnp.logical_and(last_lane, gy == n_gy - 1), 1.0, 0.5)
+    share = [yz_share * 0.5] * planes
+    share[planes - 1] = jnp.where(has_right, share[0], yz_share)
+
+    def mend_w(p):
+        for c in range(3):
+            w_ref[p + 1, c] = mend(w_ref[p + 1, c], strip_w[c], p)
+
+    def put_stress(ref, p, below, above, strip_ref):
         for r in range(6):
-            sb_ref[p, r] = spread(s_b[p][r] + s_b[p + 1][r], True)
-    arrived([P_RIGHT], [Q_LEFT])
-    for c in range(3):
-        w_ref[0, c] = jnp.where(gx == 0, 0.0, pp[c] + back(lows[0][c], True))
-        w_ref[planes + 1, c] = qq[c] + back(highs[planes][c], True)
-    for p in range(-1, planes + 1):
-        for c in range(3):
-            w_ref[p + 1, c] = mend(w_ref[p + 1, c], strip_w[c], p)
-
-    sum_bb, sum_bw, sum_ww, sum_wkw = zero, zero, zero, zero
-    for p in range(planes):
+            value = spread(below[r] + above[r], True)
+            ref[p, r] = mend(value, strip_ref[r], p) * share[p]
+
+    s_w, w_modes = {}, {}
+    sums = [zero] * 4
+
+    def modes_of_w(p):
+        w_modes[p] = [forward(w_ref[p + 1, c], True) for c in range(3)]
+
+    def w_element(p):
+        scale = er[...] if p >= planes else e_ref[p]
+        fields = pair_up(w_modes[p - 1], w_modes[p])
+        if p < planes:
+            sums[3] = sums[3] + energy(fields, scale)
+        s_w[p] = stresses(fields, scale)
+
+    def add_sums(p):
         for c in range(3):
             b, w = b_ref[p, c], w_ref[p + 1, c]
-            sum_bb = sum_bb + b * b
-            sum_bw = sum_bw + b * w
-            sum_ww = sum_ww + w * w
-    s_w = {}
-    low = [forward(w_ref[0, c], True) for c in range(3)]
-    for p in range(planes + 1):
-        high = [forward(w_ref[p + 1, c], True) for c in range(3)]
-        scale = er[...] if p >= planes else e_ref[p]
-        fields = pair_up(low, high)
-        if p < planes:
-            sum_wkw = sum_wkw + energy(fields, scale)
-        s_w[p] = stresses(fields, scale)
-        low = high
-    sum_wkw = jnp.where(jnp.logical_and(first_lane, gy == 1), 0.0, sum_wkw)
+            sums[0] = sums[0] + b * b
+            sums[1] = sums[1] + b * w
+            sums[2] = sums[2] + w * w
+
     fields = strip_fields(strip_w)
     s_strip = stresses(fields, strip_e)
     counted = jnp.logical_and(lax.rem(lane, 16) == 8, jnp.logical_and(lane >= 32, lane < 32 + 16 * planes))
     counted = jnp.logical_and(counted, gy == 1)
-    sum_wkw = sum_wkw + jnp.where(counted, energy(fields, strip_e), 0.0)
+    strip_energy = jnp.where(counted, energy(fields, strip_e), 0.0)
+    for r in range(6):
+        ssw_ref[r] = spread(s_strip[r] + next_slot(s_strip[r]), False)
+
+    for p in range(1, planes - 1):
+        mend_w(p)
+        add_sums(p)
+        modes_of_w(p)
+    for p in range(2, planes - 1):
+        w_element(p)
+    for p in range(1, planes - 1):
+        put_stress(sb_ref, p, s_b[p], s_b[p + 1], ssb_ref)
+
+    arrived([B_RIGHT], [B_LEFT, E_LEFT])
+    do_element(0, b_modes(-1), m2[0])
+    do_element(planes, m2[planes - 1], b_modes(planes))
+    for p in (0, planes - 1):
+        raw_w(p)
+        mend_w(p)
+        add_sums(p)
+        modes_of_w(p)
+    w_element(1)
+    w_element(planes - 1)
+    for c in range(3):
+        w_ref[0, c] = back(lows[0][c], True)
+        w_ref[planes + 1, c] = back(highs[planes][c], True)
+    for p in (0, planes - 1):
+        put_stress(sb_ref, p, s_b[p], s_b[p + 1], ssb_ref)
+    for p in range(1, planes - 1):
+        put_stress(sw_ref, p, s_w[p], s_w[p + 1], ssw_ref)
+
+    arrived([P_RIGHT], [])
+    for c in range(3):
+        w_ref[0, c] = jnp.where(gx == 0, 0.0, pp[c] + w_ref[0, c])
+    mend_w(-1)
+    modes_of_w(-1)
+    w_element(0)
+    sums[3] = jnp.where(jnp.logical_and(first_lane, gy == 1), 0.0, sums[3]) + strip_energy
 
     row8 = lax.broadcasted_iota(jnp.int32, (8, width), 0)
     partial = jnp.zeros((8, width), jnp.float32)
-    for k, total in enumerate((sum_bb, sum_bw, sum_ww, sum_wkw)):
+    for k, total in enumerate(sums):
         partial = jnp.where(row8 == k, jnp.sum(total, axis=0, keepdims=True), partial)
     red[...] = partial
 
@@ -408,18 +447,14 @@
 
     each_member(send_sum)
 
-    for r in range(6):
-        ssw_ref[r] = spread(s_strip[r] + next_slot(s_strip[r]), False)
-    z_share = jnp.where(last_row, 1.0, 0.5)
-    yz_share = z_share * jnp.where(jnp.logical_and(last_lane, gy == n_gy - 1), 1.0, 0.5)
-    for p in range(planes):
-        share = yz_share * 0.5
-        if p == planes - 1:
-            share = jnp.where(has_right, share, yz_share)
-        for r in range(6):
-            value = spread(s_w[p][r] + s_w[p + 1][r], True)
-            sw_ref[p, r] = mend(value, ssw_ref[r], p) * share
-            sb_ref[p, r] = mend(sb_ref[p, r], ssb_ref[r], p) * share
+    put_stress(sw_ref, 0, s_w[0], s_w[1], ssw_ref)
+    arrived([], [Q_LEFT])
+    for c in range(3):
+        w_ref[planes + 1, c] = qq[c] + w_ref[planes + 1, c]
+    mend_w(planes)
+    modes_of_w(planes)
+    w_element(planes)
+    put_stress(sw_ref, planes - 1, s_w[planes - 1], s_w[planes], ssw_ref)
 
     pltpu.make_async_copy(slots, slots, red_recv).wait()
     total = red[...]
@@ -428,8 +463,8 @@
             total = total + slots[k]
     else:
         total = lax.fori_loop(0, n - 1, lambda k, value: value + slots[k], total)
-    sums = jnp.broadcast_to(jnp.sum(total, axis=1, keepdims=True), (8, width))
-    bb, bw, ww, wkw = (sums[k : k + 1] for k in range(4))
+    whole = jnp.broadcast_to(jnp.sum(total, axis=1, keepdims=True), (8, width))
+    bb, bw, ww, wkw = (whole[k : k + 1] for k in range(4))
     first_step = bb / bw
     norm = bb - 2.0 * first_step * bw + first_step * first_step * ww
     ratio = norm / bb
@@ -474,7 +509,7 @@
                 jax.ShapeDtypeStruct((3, rows, width), jnp.float32),
                 jax.ShapeDtypeStruct((6, rows, width), jnp.float32),
             ),
-            in_specs=[pl.BlockSpec(memory_space=pl.ANY)] * 2,
+            in_specs=[pl.BlockSpec(memory_space=pltpu.HBM)] * 2,
             out_specs=(pl.BlockSpec(memory_space=pltpu.VMEM),) * 2,
             scratch_shapes=[
                 vmem(3, rows, width),
@@ -492,8 +527,6 @@
                 vmem(2, *plane),
                 vmem(4, *plane),
                 vmem(planes + 2, 3, *plane),
-                vmem(3, *plane),
-                vmem(3, *plane),
                 vmem(planes, 6, *plane),
                 vmem(planes, 6, *plane),
                 vmem(6, *plane),

time: 22.6 us -> 22.4 us (level)
  no operation moved by 1% of the time
where the time goes in v2:
time: 22.4 us; the launch traced here: 22.2 us
  Pallas kernels  18.4 us (82%)
  local copies, waits for them, and re-layouts  3.18 us (14%)
  between operations  0.65 us (3%)
    pallas_call x1, Pallas kernels, per_device(): pl.pallas_call(functools.partial(kernel, n_gx, n_gy), out_shape=(jax.Shap...  18.4 us
    unnamed x6, local copies, waits for them, and re-layouts  3.18 us

profile of v2, /device:TPU:0, one launch (start us, length us, event | category | flops | bytes accessed | tf_op | source)
XLA Modules:
  0.0 22.2 jit_solution(16063684256217256647)
XLA Ops:
  0.6 0.0 copy-start
  0.6 0.9 %copy-done = f32[3,32,4,128]{3,2,1,0:T(4,128)S(1)} copy-done((f32[3,32,4,128]{3,2,1,0:T(4,128)S(1)}, f32[3,32,4,128]{3,2,1,0:T(4,128)}, u32[]{:S(2)}) %copy-start) | copy-done | bytes 196632
  1.6 0.0 copy-start.1
  1.6 0.8 %copy-done.1 = f32[32,4,128]{2,1,0:T(4,128)S(1)} copy-done((f32[32,4,128]{2,1,0:T(4,128)S(1)}, f32[32,4,128]{2,1,0:T(4,128)}, u32[]{:S(2)}) %copy-start.1) | copy-done | bytes 65560
  2.4 18.4 %shard_map.41 = (f32[3,128,128]{2,1,0:T(8,128)S(1)}, f32[6,128,128]{2,1,0:T(8,128)S(1)}) custom-call(f32[3,128,128]{2,1,0:T(8,128)S(1)} %bitcast.6, f32[128,128]{1,0:T(8,128)S(1)} %bitcast.7), custom_call_target="tpu_custom_call" | custom-call | tf_op jit(solution)/shard_map/pallas_call | solution.py:506
  20.8 0.7 %copy.6 = f32[3,32,4,128]{3,2,1,0:T(4,128)} copy(f32[3,32,4,128]{3,2,1,0:T(4,128)S(1)} %bitcast.5) | data formatting | bytes 393216
  21.5 0.7 %copy.7 = f32[6,32,4,128]{3,2,1,0:T(4,128)} copy(f32[6,32,4,128]{3,2,1,0:T(4,128)S(1)} %bitcast.4) | data formatting | bytes 786432
Async XLA Ops:
  0.6 0.9 %copy-start = (f32[3,32,4,128]{3,2,1,0:T(4,128)S(1)}, f32[3,32,4,128]{3,2,1,0:T(4,128)}, u32[]{:S(2)}) copy-start(f32[3,32,4,128]{3,2,1,0:T(4,128)} %param.2) | copy-start | bytes 589828
  1.6 0.8 %copy-start.1 = (f32[32,4,128]{2,1,0:T(4,128)S(1)}, f32[32,4,128]{2,1,0:T(4,128)}, u32[]{:S(2)}) copy-start(f32[32,4,128]{2,1,0:T(4,128)} %param.3) | copy-start | bytes 196612

commit v3 on v2

--- a/solution.py
+++ b/solution.py
@@ -491,6 +491,17 @@
     def _():
         for copy in to_left.values():
             copy.wait_send()
+
+
+def store(x_ref, s_ref, x_out, s_out, sem):
+    copies = [
+        pltpu.make_async_copy(x_ref, x_out, sem.at[0]),
+        pltpu.make_async_copy(s_ref, s_out, sem.at[1]),
+    ]
+    for copy in copies:
+        copy.start()
+    for copy in copies:
+        copy.wait()
 
 
 def solution(mesh):
@@ -542,7 +553,20 @@
             compiler_params=pltpu.CompilerParams(
                 collective_id=0, has_side_effects=True, vmem_limit_bytes=32 * 1024 * 1024
             ),
-        )(body_force.reshape(3, rows, width), modulus.reshape(rows, width))
+        )(
+            pltpu.with_memory_space_constraint(body_force.reshape(3, rows, width), pltpu.HBM),
+            pltpu.with_memory_space_constraint(modulus.reshape(rows, width), pltpu.HBM),
+        )
+        field, stress = pl.pallas_call(
+            store,
+            out_shape=(
+                jax.ShapeDtypeStruct((3, rows, width), jnp.float32),
+                jax.ShapeDtypeStruct((6, rows, width), jnp.float32),
+            ),
+            in_specs=[pl.BlockSpec(memory_space=pl.ANY)] * 2,
+            out_specs=(pl.BlockSpec(memory_space=pl.ANY),) * 2,
+            scratch_shapes=[pltpu.SemaphoreType.DMA((2,))],
+        )(field, stress)
         return (
             field.reshape(3, depth, planes, width),
             stress.reshape(6, depth, planes, width),

time: 22.4 us -> 39.3 us (1.75)
  Pallas kernels: 18.4 us -> 37.1 us
  local copies, waits for them, and re-layouts: 3.18 us -> 1.42 us
    pallas_call x0 -> x1, Pallas kernels: none -> 19 us  [per_device(): pl.pallas_call(store, out_shape=(jax.ShapeDtypeStruct((3, rows, width), j...]
    unnamed x6 -> x4, local copies, waits for them, and re-layouts: 3.18 us -> 1.42 us
where the time goes in v3:
time: 39.3 us; the launch traced here: 39.2 us
  Pallas kernels  37.1 us (94%)
  local copies, waits for them, and re-layouts  1.42 us (4%)
  between operations  0.65 us (2%)
    pallas_call x1, Pallas kernels, per_device(): pl.pallas_call(store, out_shape=(jax.ShapeDtypeStruct((3, rows, width), j...  19 us
    pallas_call x1, Pallas kernels, per_device(): pl.pallas_call(functools.partial(kernel, n_gx, n_gy), out_shape=(jax.Shap...  18.1 us
    unnamed x4, local copies, waits for them, and re-layouts  1.42 us

profile of v3, /device:TPU:0, one launch (start us, length us, event | category | flops | bytes accessed | tf_op | source)
XLA Modules:
  0.0 39.2 jit_solution(11724612384916630485)
XLA Ops:
  0.6 18.1 %shard_map.41 = (f32[3,128,128]{2,1,0:T(8,128)S(1)}, f32[6,128,128]{2,1,0:T(8,128)S(1)}) custom-call(f32[3,128,128]{2,1,0:T(8,128)} %bitcast.4, f32[128,128]{1,0:T(8,128)} %bitcast.5), custom_call_target="tpu_custom_call" | custom-call | tf_op jit(solution)/shard_map/pallas_call | solution.py:517
  18.8 0.0 copy-start
  18.8 0.7 %copy-done = f32[6,128,128]{2,1,0:T(8,128)} copy-done((f32[6,128,128]{2,1,0:T(8,128)}, f32[6,128,128]{2,1,0:T(8,128)S(1)}, u32[]{:S(2)}) %copy-start) | copy-done | bytes 393240
  19.5 0.0 copy-start.1
  19.5 0.7 %copy-done.1 = f32[3,128,128]{2,1,0:T(8,128)} copy-done((f32[3,128,128]{2,1,0:T(8,128)}, f32[3,128,128]{2,1,0:T(8,128)S(1)}, u32[]{:S(2)}) %copy-start.1) | copy-done | bytes 196632
  20.2 19.0 %shard_map.42 = (f32[3,128,128]{2,1,0:T(8,128)}, f32[6,128,128]{2,1,0:T(8,128)}) custom-call(f32[3,128,128]{2,1,0:T(8,128)} %copy-done.1, f32[6,128,128]{2,1,0:T(8,128)} %copy-done), custom_call_target="tpu_custom_call" | custom-call | tf_op jit(solution)/shard_map/pallas_call | solution.py:560
Async XLA Ops:
  18.8 0.8 %copy-start = (f32[6,128,128]{2,1,0:T(8,128)}, f32[6,128,128]{2,1,0:T(8,128)S(1)}, u32[]{:S(2)}) copy-start(f32[6,128,128]{2,1,0:T(8,128)S(1)} %get-tuple-element.7.s_ref) | copy-start | bytes 1179652
  19.5 0.7 %copy-start.1 = (f32[3,128,128]{2,1,0:T(8,128)}, f32[3,128,128]{2,1,0:T(8,128)S(1)}, u32[]{:S(2)}) copy-start(f32[3,128,128]{2,1,0:T(8,128)S(1)} %get-tuple-element.6.x_ref) | copy-start | bytes 589828

commit v4 on v2

--- a/solution.py
+++ b/solution.py
@@ -542,7 +542,10 @@
             compiler_params=pltpu.CompilerParams(
                 collective_id=0, has_side_effects=True, vmem_limit_bytes=32 * 1024 * 1024
             ),
-        )(body_force.reshape(3, rows, width), modulus.reshape(rows, width))
+        )(
+            pltpu.with_memory_space_constraint(body_force.reshape(3, rows, width), pltpu.HBM),
+            pltpu.with_memory_space_constraint(modulus.reshape(rows, width), pltpu.HBM),
+        )
         return (
             field.reshape(3, depth, planes, width),
             stress.reshape(6, depth, planes, width),

time: 22.4 us -> 20.3 us (0.906)
  local copies, waits for them, and re-layouts: 3.18 us -> 1.42 us
  Pallas kernels: 18.4 us -> 18.1 us
    unnamed x6 -> x2, local copies, waits for them, and re-layouts: 3.18 us -> 1.42 us
    pallas_call x1, Pallas kernels: 18.4 us -> 18.1 us  [per_device(): pl.pallas_call(functools.partial(kernel, n_gx, n_gy), out_shape=(jax.Shap...]
where the time goes in v4:
time: 20.3 us; the launch traced here: 20.2 us
  Pallas kernels  18.1 us (89%)
  local copies, waits for them, and re-layouts  1.42 us (7%)
  between operations  0.64 us (3%)
    pallas_call x1, Pallas kernels, per_device(): pl.pallas_call(functools.partial(kernel, n_gx, n_gy), out_shape=(jax.Shap...  18.1 us
    unnamed x2, local copies, waits for them, and re-layouts  1.42 us

profile of v4, /device:TPU:0, one launch (start us, length us, event | category | flops | bytes accessed | tf_op | source)
XLA Modules:
  0.0 20.2 jit_solution(11865314043145998585)
XLA Ops:
  0.6 18.1 %shard_map.41 = (f32[3,128,128]{2,1,0:T(8,128)S(1)}, f32[6,128,128]{2,1,0:T(8,128)S(1)}) custom-call(f32[3,128,128]{2,1,0:T(8,128)} %bitcast.6, f32[128,128]{1,0:T(8,128)} %bitcast.7), custom_call_target="tpu_custom_call" | custom-call | tf_op jit(solution)/shard_map/pallas_call | solution.py:506
  18.8 0.7 %copy.6 = f32[3,32,4,128]{3,2,1,0:T(4,128)} copy(f32[3,32,4,128]{3,2,1,0:T(4,128)S(1)} %bitcast.5) | data formatting | bytes 393216
  19.5 0.7 %copy.7 = f32[6,32,4,128]{3,2,1,0:T(4,128)} copy(f32[6,32,4,128]{3,2,1,0:T(4,128)S(1)} %bitcast.4) | data formatting | bytes 786432

commit v5 on v4

--- a/solution.py
+++ b/solution.py
@@ -85,7 +85,7 @@
 
 def kernel(n_gx, n_gy, f_hbm, e_hbm, x_out, s_out,
            f_in, e_in, b_ref, e_ref, bl, pp, br, er, qq, p_out, q_out,
-           msg, st_same, st_other, w_ref, sb_ref, sw_ref, ssb_ref, ssw_ref,
+           msg, st_same, st_other, w_ref, bm_ref, wm_ref, high_ref, low_ref, sbe_ref, swe_ref, sb_ref, sw_ref, ssb_ref, ssw_ref,
            red, slots, in_sem, send_sem, recv_sem, red_send, red_recv):
     gx, gy = lax.axis_index("gx"), lax.axis_index("gy")
     rows = e_hbm.shape[0]
@@ -283,31 +283,62 @@
     def b_plane(p, c):
         return bl[c] if p < 0 else br[c] if p >= planes else b_ref[p, c]
 
-    def b_modes(p):
-        return [forward(b_plane(p, c), True) for c in range(3)]
-
-    m2 = [b_modes(p) for p in range(planes)]
-    highs, lows, s_b = {}, {}, {}
-
-    def do_element(p, low, high):
-        scale = er[...] if p >= planes else e_ref[p]
-        fields = pair_up(low, high)
-        highs[p], lows[p] = forces(fields, scale)
-        s_b[p] = stresses(fields, scale)
-
-    do_element(planes - 1, m2[planes - 2], m2[planes - 1])
+    def keep_modes(ref, p, values):
+        for c in range(3):
+            for (a, d), value in forward(values[c], True).items():
+                ref[p + 1, 4 * c + 2 * a + d] = value
+
+    def keep_b_modes(p):
+        keep_modes(bm_ref, p, [b_plane(p, c) for c in range(3)])
+
+    def tile_fields(ref, p, tile):
+        def side(k):
+            return [{(a, d): ref[k, 4 * c + 2 * a + d, tile, :] for a in range(2) for d in range(2)} for c in range(3)]
+        return pair_up(side(p), side(p + 1))
+
+    def tile_scale(p, tile):
+        return er[tile, :] if p >= planes else e_ref[p, tile, :]
+
+    def tiles(body, carry):
+        return lax.fori_loop(0, depth // 8, lambda t, value: body(pl.ds(pl.multiple_of(8 * t, 8), 8), value), carry)
+
+    def keep_stress(ref, p, tile, fields, scale):
+        for r, value in enumerate(stresses(fields, scale)):
+            ref[p, r, tile, :] = value
+
+    def do_element(p):
+        def body(tile, carry):
+            fields, scale = tile_fields(bm_ref, p, tile), tile_scale(p, tile)
+            high, low = forces(fields, scale)
+            for c in range(3):
+                for a, d in high[c]:
+                    high_ref[p, 4 * c + 2 * a + d, tile, :] = high[c][a, d]
+                    low_ref[p, 4 * c + 2 * a + d, tile, :] = low[c][a, d]
+            keep_stress(sbe_ref, p, tile, fields, scale)
+            return carry
+
+        tiles(body, 0)
+
+    def kept(ref, p, c):
+        return {(a, d): ref[p, 4 * c + 2 * a + d] for a in range(2) for d in range(2)}
+
+    keep_b_modes(planes - 2)
+    keep_b_modes(planes - 1)
+    do_element(planes - 1)
     for c in range(3):
-        p_out[c] = back(highs[planes - 1][c], True)
-    do_element(1, m2[0], m2[1])
+        p_out[c] = back(kept(high_ref, planes - 1, c), True)
+    keep_b_modes(0)
+    keep_b_modes(1)
+    do_element(1)
     for c in range(3):
-        q_out[c] = back(lows[1][c], True)
+        q_out[c] = back(kept(low_ref, 1, c), True)
     start([P_RIGHT], [Q_LEFT])
     for p in range(2, planes - 1):
-        do_element(p, m2[p - 1], m2[p])
+        do_element(p)
 
     def raw_w(p):
         for c in range(3):
-            w_ref[p + 1, c] = back(add(highs[p][c], lows[p + 1][c]), True)
+            w_ref[p + 1, c] = back(add(kept(high_ref, p, c), kept(low_ref, p + 1, c)), True)
 
     for p in range(1, planes - 1):
         raw_w(p)
@@ -366,23 +397,23 @@
         for c in range(3):
             w_ref[p + 1, c] = mend(w_ref[p + 1, c], strip_w[c], p)
 
-    def put_stress(ref, p, below, above, strip_ref):
+    def put_stress(ref, p, parts, strip_ref):
         for r in range(6):
-            value = spread(below[r] + above[r], True)
+            value = spread(parts[p, r] + parts[p + 1, r], True)
             ref[p, r] = mend(value, strip_ref[r], p) * share[p]
 
-    s_w, w_modes = {}, {}
-    sums = [zero] * 4
+    sums = [zero] * 3 + [jnp.zeros((8, width), jnp.float32)]
 
     def modes_of_w(p):
-        w_modes[p] = [forward(w_ref[p + 1, c], True) for c in range(3)]
+        keep_modes(wm_ref, p, [w_ref[p + 1, c] for c in range(3)])
 
     def w_element(p):
-        scale = er[...] if p >= planes else e_ref[p]
-        fields = pair_up(w_modes[p - 1], w_modes[p])
-        if p < planes:
-            sums[3] = sums[3] + energy(fields, scale)
-        s_w[p] = stresses(fields, scale)
+        def body(tile, total):
+            fields, scale = tile_fields(wm_ref, p, tile), tile_scale(p, tile)
+            keep_stress(swe_ref, p, tile, fields, scale)
+            return total + energy(fields, scale) if p < planes else total
+
+        sums[3] = tiles(body, sums[3])
 
     def add_sums(p):
         for c in range(3):
@@ -406,11 +437,13 @@
     for p in range(2, planes - 1):
         w_element(p)
     for p in range(1, planes - 1):
-        put_stress(sb_ref, p, s_b[p], s_b[p + 1], ssb_ref)
+        put_stress(sb_ref, p, sbe_ref, ssb_ref)
 
     arrived([B_RIGHT], [B_LEFT, E_LEFT])
-    do_element(0, b_modes(-1), m2[0])
-    do_element(planes, m2[planes - 1], b_modes(planes))
+    keep_b_modes(-1)
+    keep_b_modes(planes)
+    do_element(0)
+    do_element(planes)
     for p in (0, planes - 1):
         raw_w(p)
         mend_w(p)
@@ -419,12 +452,12 @@
     w_element(1)
     w_element(planes - 1)
     for c in range(3):
-        w_ref[0, c] = back(lows[0][c], True)
-        w_ref[planes + 1, c] = back(highs[planes][c], True)
+        w_ref[0, c] = back(kept(low_ref, 0, c), True)
+        w_ref[planes + 1, c] = back(kept(high_ref, planes, c), True)
     for p in (0, planes - 1):
-        put_stress(sb_ref, p, s_b[p], s_b[p + 1], ssb_ref)
+        put_stress(sb_ref, p, sbe_ref, ssb_ref)
     for p in range(1, planes - 1):
-        put_stress(sw_ref, p, s_w[p], s_w[p + 1], ssw_ref)
+        put_stress(sw_ref, p, swe_ref, ssw_ref)
 
     arrived([P_RIGHT], [])
     for c in range(3):
@@ -432,7 +465,10 @@
     mend_w(-1)
     modes_of_w(-1)
     w_element(0)
-    sums[3] = jnp.where(jnp.logical_and(first_lane, gy == 1), 0.0, sums[3]) + strip_energy
+    first = jnp.logical_and(lax.broadcasted_iota(jnp.int32, (8, width), 1) == 0, gy == 1)
+    sums[3] = jnp.where(first, 0.0, sums[3])
+    for t in range(depth // 8):
+        sums[3] = sums[3] + strip_energy[8 * t : 8 * t + 8]
 
     row8 = lax.broadcasted_iota(jnp.int32, (8, width), 0)
     partial = jnp.zeros((8, width), jnp.float32)
@@ -447,14 +483,14 @@
 
     each_member(send_sum)
 
-    put_stress(sw_ref, 0, s_w[0], s_w[1], ssw_ref)
+    put_stress(sw_ref, 0, swe_ref, ssw_ref)
     arrived([], [Q_LEFT])
     for c in range(3):
         w_ref[planes + 1, c] = qq[c] + w_ref[planes + 1, c]
     mend_w(planes)
     modes_of_w(planes)
     w_element(planes)
-    put_stress(sw_ref, planes - 1, s_w[planes - 1], s_w[planes], ssw_ref)
+    put_stress(sw_ref, planes - 1, swe_ref, ssw_ref)
 
     pltpu.make_async_copy(slots, slots, red_recv).wait()
     total = red[...]
@@ -527,6 +563,12 @@
                 vmem(2, *plane),
                 vmem(4, *plane),
                 vmem(planes + 2, 3, *plane),
+                vmem(planes + 2, 12, *plane),
+                vmem(planes + 2, 12, *plane),
+                vmem(planes + 1, 12, *plane),
+                vmem(planes + 1, 12, *plane),
+                vmem(planes + 1, 6, *plane),
+                vmem(planes + 1, 6, *plane),
                 vmem(planes, 6, *plane),
                 vmem(planes, 6, *plane),
                 vmem(6, *plane),

time: 20.3 us -> 21 us (1.034)
  Pallas kernels: 18.1 us -> 18.8 us
    pallas_call x1, Pallas kernels: 18.1 us -> 18.8 us  [per_device(): pl.pallas_call(functools.partial(kernel, n_gx, n_gy), out_shape=(jax.Shap...]
where the time goes in v5:
time: 21 us; the launch traced here: 20.8 us
  Pallas kernels  18.8 us (90%)
  local copies, waits for them, and re-layouts  1.42 us (7%)
  between operations  0.64 us (3%)
    pallas_call x1, Pallas kernels, per_device(): pl.pallas_call(functools.partial(kernel, n_gx, n_gy), out_shape=(jax.Shap...  18.8 us
    unnamed x2, local copies, waits for them, and re-layouts  1.42 us

profile of v5, /device:TPU:0, one launch (start us, length us, event | category | flops | bytes accessed | tf_op | source)
XLA Modules:
  0.0 20.8 jit_solution(16196936312024139510)
XLA Ops:
  0.6 18.8 %shard_map.41 = (f32[3,128,128]{2,1,0:T(8,128)S(1)}, f32[6,128,128]{2,1,0:T(8,128)S(1)}) custom-call(f32[3,128,128]{2,1,0:T(8,128)} %bitcast.6, f32[128,128]{1,0:T(8,128)} %bitcast.7), custom_call_target="tpu_custom_call" | custom-call | tf_op jit(solution)/shard_map/pallas_call | solution.py:542
  19.4 0.7 %copy.6 = f32[3,32,4,128]{3,2,1,0:T(4,128)} copy(f32[3,32,4,128]{3,2,1,0:T(4,128)S(1)} %bitcast.5) | data formatting | bytes 393216
  20.1 0.7 %copy.7 = f32[6,32,4,128]{3,2,1,0:T(4,128)} copy(f32[6,32,4,128]{3,2,1,0:T(4,128)S(1)} %bitcast.4) | data formatting | bytes 786432

commit v6 on v3

--- a/solution.py
+++ b/solution.py
@@ -495,8 +495,8 @@
 
 def store(x_ref, s_ref, x_out, s_out, sem):
     copies = [
+        pltpu.make_async_copy(s_ref, s_out, sem.at[1]),
         pltpu.make_async_copy(x_ref, x_out, sem.at[0]),
-        pltpu.make_async_copy(s_ref, s_out, sem.at[1]),
     ]
     for copy in copies:
         copy.start()
@@ -564,8 +564,9 @@
                 jax.ShapeDtypeStruct((6, rows, width), jnp.float32),
             ),
             in_specs=[pl.BlockSpec(memory_space=pl.ANY)] * 2,
-            out_specs=(pl.BlockSpec(memory_space=pl.ANY),) * 2,
+            out_specs=(pl.BlockSpec(memory_space=pltpu.HBM),) * 2,
             scratch_shapes=[pltpu.SemaphoreType.DMA((2,))],
+            compiler_params=pltpu.CompilerParams(vmem_limit_bytes=4 * 1024 * 1024),
         )(field, stress)
         return (
             field.reshape(3, depth, planes, width),

time: 39.3 us -> 19.7 us (0.50)
  Pallas kernels: 37.1 us -> 19 us
  local copies, waits for them, and re-layouts: 1.42 us -> 0 us
    pallas_call x1, Pallas kernels: 19 us -> 0.83 us  [per_device(): pl.pallas_call(store, out_shape=(jax.ShapeDtypeStruct((3, rows, width), j...]
    unnamed x4 -> x0, local copies, waits for them, and re-layouts: 1.42 us -> none
where the time goes in v6:
time: 19.7 us; the launch traced here: 19.6 us
  Pallas kernels  19 us (96%)
  between operations  0.64 us (3%)
    pallas_call x1, Pallas kernels, per_device(): pl.pallas_call(functools.partial(kernel, n_gx, n_gy), out_shape=(jax.Shap...  18.1 us
    pallas_call x1, Pallas kernels, per_device(): pl.pallas_call(store, out_shape=(jax.ShapeDtypeStruct((3, rows, width), j...  0.83 us

profile of v6, /device:TPU:0, one launch (start us, length us, event | category | flops | bytes accessed | tf_op | source)
XLA Modules:
  0.0 19.6 jit_solution(7164728726682571316)
XLA Ops:
  0.6 18.1 %shard_map.41 = (f32[3,128,128]{2,1,0:T(8,128)S(1)}, f32[6,128,128]{2,1,0:T(8,128)S(1)}) custom-call(f32[3,128,128]{2,1,0:T(8,128)} %bitcast.4, f32[128,128]{1,0:T(8,128)} %bitcast.5), custom_call_target="tpu_custom_call" | custom-call | tf_op jit(solution)/shard_map/pallas_call | solution.py:517
  18.8 0.8 %shard_map.42 = (f32[3,128,128]{2,1,0:T(8,128)}, f32[6,128,128]{2,1,0:T(8,128)}) custom-call(f32[3,128,128]{2,1,0:T(8,128)S(1)} %get-tuple-element.6.x_ref, f32[6,128,128]{2,1,0:T(8,128)S(1)} %get-tuple-element.7.s_ref), custom_call_target="tpu_custom_call" | custom-call | tf_op jit(solution)/shard_map/pallas_call | solution.py:560
